TPU v7x, 512 devices: a whole 4x4x16 slice. The times are simulated.
512 devices in a mesh: pipe: 4 (over z_hi), dp: 16 (over y, x), tensor: 8 (over z_lo, core).
Axes of the slice: x: 4, y: 4, z: 16 (z_hi: 4, z_lo: 4; z = z_hi * 4 + z_lo), core: 2. Of those that a mesh axis runs over, the one named last changes fastest.
Arguments:
- x_in: bfloat16 [4, 2, 16, 128, 1600], P('pipe', None, 'dp', 'tensor'), may hold values from -6 to 6
- out_grad: bfloat16 [2, 16, 128, 1600], P(None, 'dp'), may hold values from -6 to 6
- layer_scale: float32 [4, 1600], P('pipe'), may hold values from 0.05 to 1
- norm_gain: float32 [4, 1600], P('pipe'), may hold values from 0.5 to 1.5
- master: float32 [4, 1600, 8192], P('pipe', 'dp', 'tensor'), may hold values from -0.15625 to 0.15625
- moment_one: float32 [4, 1600, 8192], P('pipe', 'dp', 'tensor'), may hold values from -4 to 4
- moment_two: float32 [4, 1600, 8192], P('pipe', 'dp', 'tensor'), may hold values from 0.05 to 5
Outputs:
- input_grads: bfloat16 [4, 2, 16, 128, 1600], P('pipe', None, 'dp', 'tensor')
- new_master: float32 [4, 1600, 8192], P('pipe', 'dp', 'tensor')
- new_moment_one: float32 [4, 1600, 8192], P('pipe', 'dp', 'tensor')
- new_moment_two: float32 [4, 1600, 8192], P('pipe', 'dp', 'tensor')
- scale_grads: float32 [4, 2, 1600], P('pipe')
All inputs are finite; a program needn't handle non-finite values.
Results may differ from a plain program's by a relative error of at most 0.027.
Values may be sent and summed in bfloat16 or wider, within the bound.
A program may use at most 128 MiB of HBM per device.

v0:
```python
import math
import jax
import jax.numpy as jnp
from jax import lax
from jax.sharding import PartitionSpec as P

HD = 128
beta_one = 0.9
beta_two = 0.95
adam_eps = 1e-08
learn_rate = 0.001
weight_decay = 0.05
adam_step = 100.0
norm_eps = 1e-06


def from_behind(block, axis, distance):
    devices = range(lax.axis_size(axis))
    route = [(i - distance, i) for i in devices if i - distance in devices]
    return lax.ppermute(block, axis, route)


def normalize(values_in):
    inverse = lax.rsqrt(jnp.mean(values_in * values_in, axis=-1, keepdims=True) + norm_eps)
    return (inverse, values_in * inverse)


def select_micro(array, micro_index):
    return lax.dynamic_index_in_dim(array, micro_index, 0, keepdims=False)


def store_slot(buffer, value, slot_index):
    return lax.dynamic_update_index_in_dim(buffer, value, slot_index, 0)


def local(x_in, out_grad, layer_scale, norm_gain, master, moment_one, moment_two):
    n_pipe = lax.axis_size("pipe")
    n_tensor = lax.axis_size("tensor")
    pipe_rank = lax.axis_index("pipe")
    micro_count = x_in.shape[1]
    images = x_in.shape[2]
    shard_len = x_in.shape[3]
    channels = x_in.shape[4]
    seq_len = shard_len * n_tensor
    row_start = lax.axis_index("tensor") * shard_len
    head_cols = master.shape[2] // 4
    local_heads = head_cols // HD
    score_root = math.sqrt(HD)
    scale_vec = layer_scale[0]
    gain_vec = norm_gain[0]
    weights = lax.all_gather(master[0].astype(jnp.bfloat16), "dp", axis=0, tiled=True)
    w_qkv = weights[:, : 3 * head_cols]
    w_out = weights[:, 3 * head_cols :]
    full_x = lax.all_gather(x_in[0], "tensor", axis=2, tiled=True).astype(jnp.float32)
    full_inverse, full_unit = normalize(full_x)
    normed = (full_unit * gain_vec).astype(jnp.bfloat16)
    local_unit = lax.dynamic_slice_in_dim(full_unit, row_start, shard_len, 2)
    local_inverse = lax.dynamic_slice_in_dim(full_inverse, row_start, shard_len, 2)
    projected = jnp.einsum(
        "mbsd,dc->mbsc", normed, w_qkv, preferred_element_type=jnp.float32
    ).astype(jnp.bfloat16)
    projected = projected.reshape(micro_count, images, seq_len, 3, local_heads, HD)
    query = projected[:, :, :, 0]
    keys = projected[:, :, :, 1]
    values = projected[:, :, :, 2]
    scores = (
        jnp.einsum("mbqhe,mbkhe->mbhqk", query, keys, preferred_element_type=jnp.float32)
        / score_root
    )
    probs = jax.nn.softmax(scores, axis=-1)
    probs_low = probs.astype(jnp.bfloat16)
    attended = jnp.einsum(
        "mbhqk,mbkhe->mbqhe", probs_low, values, preferred_element_type=jnp.float32
    ).astype(jnp.bfloat16)
    attended_flat = attended.reshape(micro_count, images, seq_len, head_cols)

    def backward_segment(micro_index, incoming):
        query_now = select_micro(query, micro_index)
        keys_now = select_micro(keys, micro_index)
        values_now = select_micro(values, micro_index)
        probs_now = select_micro(probs, micro_index)
        probs_low_now = select_micro(probs_low, micro_index)
        attended_now = select_micro(attended, micro_index)
        scaled = (scale_vec * incoming.astype(jnp.float32)).astype(jnp.bfloat16)
        d_att = jnp.einsum("bsd,dc->bsc", scaled, w_out, preferred_element_type=jnp.float32).astype(
            jnp.bfloat16
        )
        d_att = d_att.reshape(images, seq_len, local_heads, HD)
        d_prob = jnp.einsum(
            "bqhe,bkhe->bhqk", d_att, values_now, preferred_element_type=jnp.float32
        )
        row_delta = jnp.einsum(
            "bqhe,bqhe->bhq", d_att, attended_now, preferred_element_type=jnp.float32
        )
        d_score = (probs_now * (d_prob - row_delta[..., None]) / score_root).astype(jnp.bfloat16)
        d_query = jnp.einsum(
            "bhqk,bkhe->bqhe", d_score, keys_now, preferred_element_type=jnp.float32
        ).astype(jnp.bfloat16)
        d_keys = jnp.einsum(
            "bhqk,bqhe->bkhe", d_score, query_now, preferred_element_type=jnp.float32
        ).astype(jnp.bfloat16)
        d_values = jnp.einsum(
            "bhqk,bqhe->bkhe", probs_low_now, d_att, preferred_element_type=jnp.float32
        ).astype(jnp.bfloat16)
        d_proj = jnp.concatenate([d_query, d_keys, d_values], axis=2).reshape(
            images, seq_len, 3 * head_cols
        )
        partial_sum = jnp.einsum("bsc,dc->bsd", d_proj, w_qkv, preferred_element_type=jnp.float32)
        return (partial_sum, d_proj, scaled)

    def spare_segment(micro_index, incoming):
        return (
            jnp.zeros((images, seq_len, channels), jnp.float32),
            jnp.zeros((images, seq_len, 3 * head_cols), jnp.bfloat16),
            jnp.zeros((images, seq_len, channels), jnp.bfloat16),
        )

    segments = n_pipe + micro_count - 1
    is_last = pipe_rank == n_pipe - 1
    received = jnp.zeros((images, seq_len, channels), jnp.bfloat16)
    slots = micro_count + 1
    grads_out = jnp.zeros((slots, images, shard_len, channels), jnp.bfloat16)
    proj_saved = jnp.zeros((slots, images, seq_len, 3 * head_cols), jnp.bfloat16)
    scaled_saved = jnp.zeros((slots, images, seq_len, channels), jnp.bfloat16)
    grad_saved = jnp.zeros((slots, images, seq_len, channels), jnp.bfloat16)
    gain_part = jnp.zeros((channels,), jnp.float32)
    for segment_step in range(segments):
        micro_index = segment_step - (n_pipe - 1) + pipe_rank
        active = jnp.logical_and(micro_index >= 0, micro_index < micro_count)
        micro_index = jnp.clip(micro_index, 0, micro_count - 1)
        slot_index = jnp.where(active, micro_index, micro_count)
        arrived = received
        incoming = jnp.where(is_last, select_micro(out_grad, micro_index), arrived)
        partial_sum, d_proj, scaled = lax.cond(
            active, backward_segment, spare_segment, micro_index, incoming
        )
        pieces = partial_sum.astype(jnp.bfloat16).reshape(images, n_tensor, shard_len, channels)
        landed = lax.all_to_all(pieces, "tensor", split_axis=1, concat_axis=1, tiled=True)
        own_d = jnp.sum(landed.astype(jnp.float32), axis=1)
        own_unit = select_micro(local_unit, micro_index)
        own_inverse = select_micro(local_inverse, micro_index)
        d_unit = own_d * gain_vec
        d_input = own_inverse * (
            d_unit - own_unit * jnp.mean(d_unit * own_unit, axis=-1, keepdims=True)
        )
        own_incoming = lax.dynamic_slice_in_dim(incoming, row_start, shard_len, 1)
        own_passed = (own_incoming.astype(jnp.float32) + d_input).astype(jnp.bfloat16)
        gain_part = gain_part + jnp.where(active, jnp.sum(own_d * own_unit, axis=(0, 1)), 0.0)
        grads_out = store_slot(grads_out, own_passed, slot_index)
        proj_saved = store_slot(proj_saved, d_proj, slot_index)
        scaled_saved = store_slot(scaled_saved, scaled, slot_index)
        grad_saved = store_slot(grad_saved, incoming, slot_index)
        if segment_step + 1 < segments:
            moved = from_behind(own_passed, "pipe", -1)
            received = lax.all_gather(moved, "tensor", axis=1, tiled=True)
    grads_kept = grads_out[:micro_count]
    proj_kept = proj_saved[:micro_count]
    scaled_kept = scaled_saved[:micro_count]
    grad_kept = grad_saved[:micro_count]
    grad_qkv = jnp.einsum("mbsd,mbsc->dc", normed, proj_kept, preferred_element_type=jnp.float32)
    grad_out = jnp.einsum(
        "mbsd,mbsc->dc", scaled_kept, attended_flat, preferred_element_type=jnp.float32
    )
    weight_grad = lax.psum_scatter(
        jnp.concatenate([grad_qkv, grad_out], axis=1).astype(jnp.bfloat16),
        "dp",
        scatter_dimension=0,
        tiled=True,
    ).astype(jnp.float32)
    summed_out = jnp.einsum(
        "mbsd,mbsc->dc", grad_kept, attended_flat, preferred_element_type=jnp.float32
    )
    scale_part = jnp.sum(w_out.astype(jnp.float32) * summed_out, axis=1)
    scale_both = lax.psum(lax.psum(jnp.stack([scale_part, gain_part]), "tensor"), "dp")
    bias_one = 1.0 - beta_one**adam_step
    bias_two = 1.0 - beta_two**adam_step
    first_new = beta_one * moment_one[0] + (1.0 - beta_one) * weight_grad
    second_new = beta_two * moment_two[0] + (1.0 - beta_two) * weight_grad * weight_grad
    update = first_new / bias_one / (jnp.sqrt(second_new / bias_two) + adam_eps)
    master_new = master[0] - learn_rate * (update + weight_decay * master[0])
    return (grads_kept[None], master_new[None], first_new[None], second_new[None], scale_both[None])


def solution(mesh):
    placed = (
        P("pipe", None, "dp", "tensor", None),
        P(None, "dp", None, None),
        P("pipe", None),
        P("pipe", None),
        P("pipe", "dp", "tensor"),
        P("pipe", "dp", "tensor"),
        P("pipe", "dp", "tensor"),
    )
    return jax.shard_map(
        local,
        mesh=mesh,
        in_specs=placed,
        out_specs=(
            P("pipe", None, "dp", "tensor", None),
            P("pipe", "dp", "tensor"),
            P("pipe", "dp", "tensor"),
            P("pipe", "dp", "tensor"),
            P("pipe", None, None),
        ),
        check_vma=False,
    )
```

profile of v0, /device:TPU:128, one launch (start us, length us, event | category | flops | bytes accessed | tf_op | source)
XLA Modules:
  0.0 831.2 jit_solution(14182584001447104835)
XLA Ops:
  9.8 17.2 %all-gather = bf16[1,2,1,128,1600]{4,3,2,1,0:T(8,128)(2,1)S(1)} all-gather(bf16[1,2,1,16,1600]{4,3,2,1,0:T(8,128)(2,1)} %param.17), channel_id=2, replica_groups=mesh['pipe'=4,'dp'=16,'tensor'=8] {'tensor'}, dimensions={3}, use_global_device_ids=true | all-gather | bytes 921600 | tf_op jit(solution)/shard_map/all_gather | solution.py:54
  28.4 50.3 %all-gather.4.cloned.1.call-done = bf16[16,100,1024]{2,1,0:T(8,128)(2,1)} async-done(((bf16[1,100,1024]{2,1,0:T(8,128)(2,1)}), bf16[16,100,1024]{2,1,0:T(8,128)(2,1)}) %all-gather.4.cloned.1.call-update) | async-done | bytes 3276816 | tf_op jit(solution)/shard_map/all_gather | solution.py:51
  78.8 4.5 reshape.1362
  84.5 2.6 fusion.115
  91.8 2.1 convolution_convert_fusion.20
  95.5 2.3 conditional.5
  97.8 2.0 copy.213
  99.8 4.8 all-to-all-start
  106.1 2.5 convert_multiply_fusion.6
  108.6 9.3 %all-to-all-done = bf16[1,8,16,1600]{3,2,0,1:T(8,128)(2,1)} async-done(((bf16[1,8,16,1600]{3,2,0,1:T(8,128)(2,1)}), bf16[1,8,16,1600]{3,2,0,1:T(8,128)(2,1)}, u32[]{:S(2)}, u32[]{:S(2)}) %all-to-all-start) | async-done | bytes 409632 | tf_op jit(solution)/shard_map/all_to_all | solution.py:138
  119.7 2.1 copy.216
  121.8 2.2 fusion.165
  124.0 2.1 copy.217
  128.0 2.2 fusion.121
  130.1 2.1 collective-permute-start
  132.2 40.1 %collective-permute-done = bf16[1,16,1600]{1,2,0:T(8,128)(2,1)} collective-permute-done((bf16[1,16,1600]{1,2,0:T(8,128)(2,1)}, bf16[1,16,1600]{1,2,0:T(8,128)(2,1)}, u32[]{:S(2)}, u32[]{:S(2)}) %collective-permute-start) | collective-permute-done | bytes 51232 | tf_op jit(solution)/shard_map/ppermute | solution.py:20
  174.1 15.8 %all_gather.20 = bf16[1,128,1600]{2,1,0:T(8,128)(2,1)} all-gather(bf16[1,16,1600]{2,1,0:T(8,128)(2,1)} %copy.219), channel_id=1, replica_groups=mesh['pipe'=4,'dp'=16,'tensor'=8] {'tensor'}, dimensions={1}, use_global_device_ids=true | all-gather | bytes 460800 | tf_op jit(solution)/shard_map/all_gather | solution.py:155
  191.9 2.1 bitcast_dynamic-update-slice_fusion.2
  194.0 2.7 conditional.6
  196.8 2.0 copy.228
  198.7 16.6 %all_to_all.25 = bf16[1,8,16,1600]{3,2,0,1:T(8,128)(2,1)S(1)} all-to-all(bf16[1,8,16,1600]{3,2,0,1:T(8,128)(2,1)} %bitcast.592), channel_id=1, replica_groups=mesh['pipe'=4,'dp'=16,'tensor'=8] {'tensor'}, dimensions={1} | all-to-all | bytes 819200 | tf_op jit(solution)/shard_map/all_to_all | solution.py:138
  216.1 2.2 fusion.164
  218.2 2.1 copy.231
  220.3 2.1 copy.232
  224.3 2.2 fusion.141
  226.4 2.2 collective-permute-start.1
  228.6 94.0 %collective-permute-done.1 = bf16[1,16,1600]{1,2,0:T(8,128)(2,1)} collective-permute-done((bf16[1,16,1600]{1,2,0:T(8,128)(2,1)}, bf16[1,16,1600]{1,2,0:T(8,128)(2,1)}, u32[]{:S(2)}, u32[]{:S(2)}) %collective-permute-start.1) | collective-permute-done | bytes 51232 | tf_op jit(solution)/shard_map/ppermute | solution.py:20
  324.4 15.8 %all_gather.21 = bf16[1,128,1600]{2,1,0:T(8,128)(2,1)} all-gather(bf16[1,16,1600]{2,1,0:T(8,128)(2,1)} %copy.234), channel_id=1, replica_groups=mesh['pipe'=4,'dp'=16,'tensor'=8] {'tensor'}, dimensions={1}, use_global_device_ids=true | all-gather | bytes 460800 | tf_op jit(solution)/shard_map/all_gather | solution.py:155
  342.2 2.1 bitcast_dynamic-update-slice_fusion.1
  344.3 32.0 %conditional.7 = (bf16[1,128,1600]{1,2,0:T(8,128)(2,1)}, bf16[1,1,128,768]{3,2,0,1:T(8,128)(2,1)}, bf16[1,1,128,1600]{2,3,0,1:T(8,128)(2,1)}) conditional(s32[]{:T(128)} %convert_element_type.339, () %tuple.72, (s32[]{:T(128)}, bf16[2,1,128,2,128]{4,2,3,0,1:T(8,128)(2,1)}, f32[2,1,2,128,128]{3,4,2,0,1:T(8,128)S(1)}, f32[1,1600]{1,0:T(1,128)S(1)}, ...), branch_computations={%region_11.12_spmd, %region_12.13_spmd} | conditional | flops 454803200 | bytes 11565162 | solution.py:134
  354.1 2.0 copy.238
  359.9 1.9 copy.357
  376.4 2.0 copy.243
  378.3 4.1 all-to-all-start.2
  391.7 4.0 all-to-all-done.2
  397.4 2.2 fusion.163
  399.6 2.1 copy.246
  401.7 2.2 copy.247
  411.1 38.8 %collective-permute-done.2 = bf16[1,16,1600]{1,2,0:T(8,128)(2,1)} collective-permute-done((bf16[1,16,1600]{1,2,0:T(8,128)(2,1)S(1)}, bf16[1,16,1600]{1,2,0:T(8,128)(2,1)}, u32[]{:S(2)}, u32[]{:S(2)}) %collective-permute-start.2) | collective-permute-done | bytes 51232 | tf_op jit(solution)/shard_map/ppermute | solution.py:20
  451.8 15.8 %all_gather.22 = bf16[1,128,1600]{2,1,0:T(8,128)(2,1)} all-gather(bf16[1,16,1600]{2,1,0:T(8,128)(2,1)} %copy.249), channel_id=1, replica_groups=mesh['pipe'=4,'dp'=16,'tensor'=8] {'tensor'}, dimensions={1}, use_global_device_ids=true | all-gather | bytes 460800 | tf_op jit(solution)/shard_map/all_gather | solution.py:155
  469.5 2.1 bitcast_dynamic-update-slice_fusion
  471.6 32.2 %conditional.8 = (bf16[1,128,1600]{1,2,0:T(8,128)(2,1)}, bf16[1,1,128,768]{3,2,0,1:T(8,128)(2,1)}, bf16[1,1,128,1600]{2,3,0,1:T(8,128)(2,1)}) conditional(s32[]{:T(128)} %convert_element_type.344, () %tuple.74, (s32[]{:T(128)}, bf16[2,1,128,2,128]{4,2,3,0,1:T(8,128)(2,1)}, f32[2,1,2,128,128]{3,4,2,0,1:T(8,128)S(1)}, f32[1,1600]{1,0:T(1,128)S(1)}, ...), branch_computations={%region_15.16_spmd, %region_16.17_spmd} | conditional | flops 454803200 | bytes 11565162 | solution.py:134
  481.6 2.0 copy.253
  487.4 2.0 copy.361
  503.9 2.0 copy.258
  505.9 4.1 all-to-all-start.3
  528.4 2.2 fusion.162
  530.6 2.1 copy.261
  532.7 2.2 copy.262
  536.7 2.2 fusion.131
  538.9 2.2 collective-permute-start.3
  544.3 14.5 %collective-permute-done.3 = bf16[1,16,1600]{1,2,0:T(8,128)(2,1)} collective-permute-done((bf16[1,16,1600]{1,2,0:T(8,128)(2,1)}, bf16[1,16,1600]{1,2,0:T(8,128)(2,1)}, u32[]{:S(2)}, u32[]{:S(2)}) %collective-permute-start.3) | collective-permute-done | bytes 51232 | tf_op jit(solution)/shard_map/ppermute | solution.py:20
  560.6 37.5 %all_gather.23 = bf16[1,128,1600]{2,1,0:T(8,128)(2,1)} all-gather(bf16[1,16,1600]{2,1,0:T(8,128)(2,1)} %copy.264), channel_id=1, replica_groups=mesh['pipe'=4,'dp'=16,'tensor'=8] {'tensor'}, dimensions={1}, use_global_device_ids=true | all-gather | bytes 460800 | tf_op jit(solution)/shard_map/all_gather | solution.py:155
  600.0 2.1 bitcast_dynamic-update-slice_fusion.3
  602.1 2.3 conditional.9
  604.4 2.1 copy.273
  606.5 5.1 all-to-all-start.4
  613.2 1.9 bitcast_convert_fusion
  619.0 85.0 %fusion = bf16[112,1024]{1,0:T(8,128)(2,1)} fusion(bf16[1600,1024]{1,0:T(8,128)(2,1)S(1)} %pad_maximum_fusion.5), kind=kCustom, calls=%all-reduce-scatter | all-reduce-scatter fusion | flops 1835009 | bytes 3508224
  705.0 3.7 collective-permute-start.4
  708.6 4.1 collective-permute-start.5
  712.8 2.0 fusion.114
  722.6 27.0 %psum.14 = f32[2,1600]{1,0:T(2,128)S(1)} all-reduce(f32[2,1600]{1,0:T(2,128)S(1)} %pad_maximum_fusion.6), channel_id=1, replica_groups=mesh['pipe'=4,'dp'=16,'tensor'=8] {'tensor'}, use_global_device_ids=true, to_apply=%region_30.31 | all-reduce | flops 3200 | bytes 25600 | tf_op jit(solution)/shard_map/psum | solution.py:174
  749.6 71.2 %psum.15 = f32[1,2,1600]{2,1,0:T(2,128)} all-reduce(f32[1,2,1600]{2,1,0:T(2,128)S(1)} %bitcast.594), channel_id=1, replica_groups=mesh['pipe'=4,'dp'=16,'tensor'=8] {'dp'}, use_global_device_ids=true, to_apply=%region_31.32 | all-reduce | flops 3200 | bytes 25600 | tf_op jit(solution)/shard_map/psum | solution.py:174
  (208 shorter events, 155.7 us)
Async XLA Ops:
  7.2 71.6 %all-gather.4.cloned.1.call-start = ((), (), s32[]{:S(2)}) async-start(), calls=%async_computation.5 | async-start | bytes 3620864 | tf_op jit(solution)/shard_map/all_gather | solution.py:51
  9.0 18.5 %copy-start.10 = (bf16[2,1,128,1600]{2,3,1,0:T(8,128)(2,1)S(1)}, bf16[2,1,128,1600]{2,3,1,0:T(8,128)(2,1)}, u32[]{:S(2)}) copy-start(bf16[2,1,128,1600]{2,3,1,0:T(8,128)(2,1)} %param.18) | copy-start | bytes 2457604
  27.0 57.4 %copy-start = (bf16[1,2,1,128,1600]{4,3,2,1,0:T(8,128)(2,1)}, bf16[1,2,1,128,1600]{4,3,2,1,0:T(8,128)(2,1)S(1)}, u32[]{:S(2)}) copy-start(bf16[1,2,1,128,1600]{4,3,2,1,0:T(8,128)(2,1)S(1)} %all-gather) | copy-start | bytes 2457604
  27.3 57.2 %copy-start.39 = (f32[2,128]{1,0:T(2,128)}, f32[2,128]{1,0:T(2,128)S(1)}, u32[]{:S(2)}) copy-start(f32[2,128]{1,0:T(2,128)S(1)} %add_rsqrt_fusion) | copy-start | bytes 3076
  28.4 50.4 %copy-start.21 = (bf16[3,1,128,1600]{2,3,0,1:T(8,128)(2,1)}, bf16[3,1,128,1600]{2,3,0,1:T(8,128)(2,1)S(1)}, u32[]{:S(2)}) copy-start(bf16[3,1,128,1600]{2,3,0,1:T(8,128)(2,1)S(1)} %get-tuple-element.409) | copy-start | bytes 3686404
  87.5 0.8 copy-start.27
  87.5 4.2 copy-start.26
  91.7 3.9 copy-start.33
  91.8 2.1 copy-start.12
  99.8 18.2 %all-to-all-start = ((bf16[1,8,16,1600]{3,2,0,1:T(8,128)(2,1)}), bf16[1,8,16,1600]{3,2,0,1:T(8,128)(2,1)}, u32[]{:S(2)}, u32[]{:S(2)}) async-start(bf16[1,8,16,1600]{3,2,0,1:T(8,128)(2,1)} %bitcast.589), calls=%async_computation | async-start | bytes 851968 | tf_op jit(solution)/shard_map/all_to_all | solution.py:138
  126.1 1.8 copy-start.2
  126.1 1.9 copy-start.6
  130.1 42.2 %collective-permute-start = (bf16[1,16,1600]{1,2,0:T(8,128)(2,1)}, bf16[1,16,1600]{1,2,0:T(8,128)(2,1)}, u32[]{:S(2)}, u32[]{:S(2)}) collective-permute-start(bf16[1,16,1600]{1,2,0:T(8,128)(2,1)} %fusion.121), channel_id=1, source_target_pairs={{128,0},{256,128},{384,256},{129,1},{257,129},{385,257},{130,2},{2... | collective-permute-start | bytes 153608 | tf_op jit(solution)/shard_map/ppermute | solution.py:20
  215.4 0.7 copy-start.22
  222.4 1.8 copy-start.3
  222.4 1.9 copy-start.7
  226.4 96.2 %collective-permute-start.1 = (bf16[1,16,1600]{1,2,0:T(8,128)(2,1)}, bf16[1,16,1600]{1,2,0:T(8,128)(2,1)}, u32[]{:S(2)}, u32[]{:S(2)}) collective-permute-start(bf16[1,16,1600]{1,2,0:T(8,128)(2,1)} %fusion.141), channel_id=1, source_target_pairs={{128,0},{256,128},{384,256},{129,1},{257,129},{385,257},{130,2},{2... | collective-permute-start | bytes 153608 | tf_op jit(solution)/shard_map/ppermute | solution.py:20
  372.3 0.7 copy-start.16
  378.3 17.4 %all-to-all-start.2 = ((bf16[1,8,16,1600]{3,2,0,1:T(8,128)(2,1)}), bf16[1,8,16,1600]{3,2,0,1:T(8,128)(2,1)}, u32[]{:S(2)}, u32[]{:S(2)}) async-start(bf16[1,8,16,1600]{3,2,0,1:T(8,128)(2,1)} %bitcast.590), calls=%async_computation.2 | async-start | bytes 851968 | tf_op jit(solution)/shard_map/all_to_all | solution.py:138
  396.8 0.6 copy-start.23
  403.9 1.8 copy-start.4
  403.9 1.9 copy-start.8
  405.7 4.8 copy-start.32
  407.2 0.8 copy-start.18
  407.9 42.0 %collective-permute-start.2 = (bf16[1,16,1600]{1,2,0:T(8,128)(2,1)S(1)}, bf16[1,16,1600]{1,2,0:T(8,128)(2,1)}, u32[]{:S(2)}, u32[]{:S(2)}) collective-permute-start(bf16[1,16,1600]{1,2,0:T(8,128)(2,1)S(1)} %fusion.136), channel_id=1, source_target_pairs={{128,0},{256,128},{384,256},{129,1},{257,129},{385,257},{130,2},{2... | collective-permute-start | bytes 153608 | tf_op jit(solution)/shard_map/ppermute | solution.py:20
  499.9 0.7 copy-start.17
  505.9 20.8 %all-to-all-start.3 = ((bf16[1,8,16,1600]{3,2,0,1:T(8,128)(2,1)}), bf16[1,8,16,1600]{3,2,0,1:T(8,128)(2,1)}, u32[]{:S(2)}, u32[]{:S(2)}) async-start(bf16[1,8,16,1600]{3,2,0,1:T(8,128)(2,1)} %bitcast.591), calls=%async_computation.3 | async-start | bytes 851968 | tf_op jit(solution)/shard_map/all_to_all | solution.py:138
  527.8 0.6 copy-start.24
  534.8 1.8 copy-start.5
  534.8 1.9 copy-start.9
  538.9 19.9 %collective-permute-start.3 = (bf16[1,16,1600]{1,2,0:T(8,128)(2,1)}, bf16[1,16,1600]{1,2,0:T(8,128)(2,1)}, u32[]{:S(2)}, u32[]{:S(2)}) collective-permute-start(bf16[1,16,1600]{1,2,0:T(8,128)(2,1)} %fusion.131), channel_id=1, source_target_pairs={{128,0},{256,128},{384,256},{129,1},{257,129},{385,257},{130,2},{2... | collective-permute-start | bytes 153608 | tf_op jit(solution)/shard_map/ppermute | solution.py:20
  604.4 8.8 %copy-start.1 = (bf16[1,2,1,128,1600]{4,3,2,1,0:T(8,128)(2,1)S(1)}, bf16[1,2,1,128,1600]{4,3,2,1,0:T(8,128)(2,1)}, u32[]{:S(2)}) copy-start(bf16[1,2,1,128,1600]{4,3,2,1,0:T(8,128)(2,1)} %copy-done) | copy-start | bytes 2457604
  604.4 8.8 %copy-start.40 = (f32[2,128]{1,0:T(2,128)S(1)}, f32[2,128]{1,0:T(2,128)}, u32[]{:S(2)}) copy-start(f32[2,128]{1,0:T(2,128)} %copy-done.39) | copy-start | bytes 3076
  606.5 113.7 %all-to-all-start.4 = ((bf16[1,8,16,1600]{3,2,0,1:T(8,128)(2,1)}), bf16[1,8,16,1600]{3,2,0,1:T(8,128)(2,1)}, u32[]{:S(2)}, u32[]{:S(2)}) async-start(bf16[1,8,16,1600]{3,2,0,1:T(8,128)(2,1)} %bitcast.152), calls=%async_computation.4 | async-start | bytes 851968 | tf_op jit(solution)/shard_map/all_to_all | solution.py:138
  613.2 3.7 copy-start.11
  704.0 11.5 %copy-start.20 = (bf16[112,1024]{1,0:T(8,128)(2,1)S(1)}, bf16[112,1024]{1,0:T(8,128)(2,1)}, u32[]{:S(2)}) copy-start(bf16[112,1024]{1,0:T(8,128)(2,1)} %fusion) | copy-start | bytes 688132
  705.0 10.5 %collective-permute-start.4 = (bf16[112,1024]{1,0:T(8,128)(2,1)}, bf16[112,1024]{1,0:T(8,128)(2,1)S(1)}, u32[]{:S(2)}, u32[]{:S(2)}) collective-permute-start(bf16[112,1024]{1,0:T(8,128)(2,1)} %fusion), channel_id=1, source_target_pairs={{0,8},{8,16},{16,24},{24,32},{32,40},{40,48},{48,56},{56,64},{64,7... | collective-permute-start | bytes 688136
  708.6 6.8 collective-permute-start.5
  712.7 3.4 copy-start.19
  712.7 3.4 copy-start.28
  712.7 3.4 copy-start.29
  717.8 4.7 copy-start.35
  717.8 4.7 copy-start.36
  717.8 4.7 copy-start.37
  717.8 4.7 copy-start.38
  722.2 99.2 %copy-start.13 = (bf16[1,128,1600]{1,2,0:T(8,128)(2,1)S(1)}, bf16[1,128,1600]{1,2,0:T(8,128)(2,1)}, u32[]{:S(2)}) copy-start(bf16[1,128,1600]{1,2,0:T(8,128)(2,1)} %get-tuple-element.402) | copy-start | bytes 1228804
  722.2 99.2 %copy-start.41 = (f32[16]{0:T(128)S(1)}, f32[16]{0:T(128)}, u32[]{:S(2)}) copy-start(f32[16]{0:T(128)} %get-tuple-element.429) | copy-start | bytes 196
Sparse Core Ops, SparseCore 0:
  11.6 67.1 all-gather.3
where the time goes:
time: 842 us; the launch traced here: 831 us
  blocking collectives  302 us (36%)
  waiting for transfers between devices  252 us (30%)
  local copies, waits for them, and re-layouts  145 us (17%)
  other arithmetic  54.5 us (6%)
  starting transfers between devices  34.3 us (4%)
  matrix products  27.2 us (3%)
  between operations  15.5 us (2%)
    ppermute x4, waiting for transfers between devices, from_behind(): return lax.ppermute(block, axis, route)  187 us
    unnamed x1, blocking collectives  85 us
    all_gather x4, blocking collectives, local(): received = lax.all_gather(moved, 'tensor', axis=1, tiled=True)  84.8 us
    psum x1, blocking collectives, local(): lax.psum(lax.psum(jnp.stack([scale_part, gain_part]), 'tensor'), 'dp')  71.2 us
    all_gather x1, waiting for transfers between devices, local(): lax.all_gather(master[0].astype(jnp.bfloat16), 'dp', axis=0, tiled=True)  50.3 us
    another operation x23, local copies, waits for them, and re-layouts  32.2 us
    psum x1, blocking collectives, local(): lax.psum(jnp.stack([scale_part, gain_part]), 'tensor')  27 us
    dynamic_update_slice x15, local copies, waits for them, and re-layouts, store_slot(): return lax.dynamic_update_index_in_dim(buffer, value, slot_index, 0)  22.6 us
  transfers between devices with their start and end apart: 11, of which 8 were waited for; matrix products, arithmetic and copies ran while one was open for 16% of the time, Pallas kernels for 0%

commit v1 on v0

--- a/solution.py
+++ b/solution.py
@@ -48,7 +48,25 @@
     score_root = math.sqrt(HD)
     scale_vec = layer_scale[0]
     gain_vec = norm_gain[0]
-    weights = lax.all_gather(master[0].astype(jnp.bfloat16), "dp", axis=0, tiled=True)
+    x = master[0].astype(jnp.bfloat16)
+    length, index, extent = (lax.axis_size("dp"), lax.axis_index("dp"), x.shape[0])
+    right = [(i_2, (i_2 + 1) % length) for i_2 in range(length)]
+    left = [(i_2, (i_2 - 1) % length) for i_2 in range(length)]
+    out = jnp.zeros((*x.shape[:0], length * extent, *x.shape[0 + 1 :]), x.dtype)
+    out = lax.dynamic_update_slice_in_dim(out, x, index * extent, axis=0)
+    from_left = from_right = x
+    halfway = length // 2
+    for step in range(1, halfway + 1):
+        from_left = lax.ppermute(from_left, "dp", right)
+        out = lax.dynamic_update_slice_in_dim(
+            out, from_left, (index - step) % length * extent, axis=0
+        )
+        if step < length - halfway:
+            from_right = lax.ppermute(from_right, "dp", left)
+            out = lax.dynamic_update_slice_in_dim(
+                out, from_right, (index + step) % length * extent, axis=0
+            )
+    weights = out
     w_qkv = weights[:, : 3 * head_cols]
     w_out = weights[:, 3 * head_cols :]
     full_x = lax.all_gather(x_in[0], "tensor", axis=2, tiled=True).astype(jnp.float32)

time: 842 us -> 889 us (1.056)
  starting transfers between devices: 34.3 us -> 111 us
  waiting for transfers between devices: 252 us -> 204 us
  local copies, waits for them, and re-layouts: 145 us -> 171 us
  between operations: 15.5 us -> 2.34 us
    ppermute x0 -> x15, starting transfers between devices: none -> 66.1 us  [the longest x7 49.3 us: local(): from_right = lax.ppermute(from_right, 'dp', left)]
    all_gather x1 -> x0, waiting for transfers between devices: 50.3 us -> none  [local(): lax.all_gather(master[0].astype(jnp.bfloat16), 'dp', axis=0, tiled=True)]
    dynamic_update_slice x0 -> x16, local copies, waits for them, and re-layouts: none -> 29 us  [the longest x8 14.5 us: local(): lax.dynamic_update_slice_in_dim(out, from_left, (index - step) % length *...]
    ppermute x0 -> x15, waiting for transfers between devices: none -> 11.1 us  [the longest x8 11.1 us: local(): from_left = lax.ppermute(from_left, 'dp', right)]
    ppermute x4, starting transfers between devices: 8.4 us -> 18 us  [from_behind(): return lax.ppermute(block, axis, route)]
  transfers between devices with their start and end apart: 11 -> 25, of which waited for: 8 -> 12; matrix products, arithmetic and copies ran while one was open for 16% -> 19% of each run, Pallas kernels for 0% -> 0%
where the time goes in v1:
time: 889 us; the launch traced here: 876 us
  blocking collectives  305 us (34%)
  waiting for transfers between devices  204 us (23%)
  local copies, waits for them, and re-layouts  171 us (19%)
  starting transfers between devices  111 us (12%)
  other arithmetic  55.8 us (6%)
  matrix products  27.2 us (3%)
    ppermute x4, waiting for transfers between devices, from_behind(): return lax.ppermute(block, axis, route)  180 us
    unnamed x1, blocking collectives  87.5 us
    all_gather x4, blocking collectives, local(): received = lax.all_gather(moved, 'tensor', axis=1, tiled=True)  84.8 us
    psum x1, blocking collectives, local(): lax.psum(lax.psum(jnp.stack([scale_part, gain_part]), 'tensor'), 'dp')  71 us
    ppermute x7, starting transfers between devices, local(): from_right = lax.ppermute(from_right, 'dp', left)  49.3 us
    another operation x23, local copies, waits for them, and re-layouts  33.3 us
    psum x1, blocking collectives, local(): lax.psum(jnp.stack([scale_part, gain_part]), 'tensor')  27.2 us
    dynamic_update_slice x15, local copies, waits for them, and re-layouts, store_slot(): return lax.dynamic_update_index_in_dim(buffer, value, slot_index, 0)  22.5 us
  transfers between devices with their start and end apart: 25, of which 12 were waited for; matrix products, arithmetic and copies ran while one was open for 19% of the time, Pallas kernels for 0%

profile of v1, /device:TPU:128, one launch (start us, length us, event | category | flops | bytes accessed | tf_op | source)
XLA Modules:
  0.0 876.4 jit_solution(5914497277587601556)
XLA Ops:
  1.8 3.4 collective-permute-start
  5.2 5.8 collective-permute-start.1
  11.0 3.2 collective-permute-done
  16.1 7.2 collective-permute-start.3
  23.3 2.3 collective-permute-done.2
  27.6 7.2 collective-permute-start.5
  38.6 7.2 collective-permute-start.7
  49.7 7.3 collective-permute-start.9
  60.8 17.7 %all-gather = bf16[1,2,1,128,1600]{4,3,2,1,0:T(8,128)(2,1)S(1)} all-gather(bf16[1,2,1,16,1600]{4,3,2,1,0:T(8,128)(2,1)} %param.17), channel_id=2, replica_groups=mesh['pipe'=4,'dp'=16,'tensor'=8] {'tensor'}, dimensions={3}, use_global_device_ids=true | all-gather | bytes 921600 | tf_op jit(solution)/shard_map/all_gather | solution.py:72
  78.6 7.3 collective-permute-start.11
  90.1 2.1 broadcast_in_dim.147
  94.3 7.2 collective-permute-start.13
  130.7 2.6 fusion.113
  139.2 2.1 convolution_convert_fusion.20
  142.9 2.3 conditional.5
  147.2 5.0 all-to-all-start
  153.9 2.5 convert_multiply_fusion.6
  156.4 9.2 %all-to-all-done = bf16[1,8,16,1600]{3,2,0,1:T(8,128)(2,1)} async-done(((bf16[1,8,16,1600]{3,2,0,1:T(8,128)(2,1)}), bf16[1,8,16,1600]{3,2,0,1:T(8,128)(2,1)}, u32[]{:S(2)}, u32[]{:S(2)}) %all-to-all-start) | async-done | bytes 409632 | tf_op jit(solution)/shard_map/all_to_all | solution.py:156
  167.3 2.1 copy.216
  169.4 2.2 fusion.162
  171.6 2.1 copy.217
  175.6 2.2 fusion.119
  177.7 6.9 collective-permute-start.15
  184.7 35.3 %collective-permute-done.15 = bf16[1,16,1600]{1,2,0:T(8,128)(2,1)} collective-permute-done((bf16[1,16,1600]{1,2,0:T(8,128)(2,1)}, bf16[1,16,1600]{1,2,0:T(8,128)(2,1)}, u32[]{:S(2)}, u32[]{:S(2)}) %collective-permute-start.15) | collective-permute-done | bytes 51232 | tf_op jit(solution)/shard_map/ppermute | solution.py:20
  221.8 15.8 %all_gather.16 = bf16[1,128,1600]{2,1,0:T(8,128)(2,1)} all-gather(bf16[1,16,1600]{2,1,0:T(8,128)(2,1)} %copy.219), channel_id=1, replica_groups=mesh['pipe'=4,'dp'=16,'tensor'=8] {'tensor'}, dimensions={1}, use_global_device_ids=true | all-gather | bytes 460800 | tf_op jit(solution)/shard_map/all_gather | solution.py:173
  239.5 2.2 bitcast_dynamic-update-slice_fusion.2
  241.7 2.3 conditional.6
  245.9 16.6 %all_to_all.25 = bf16[1,8,16,1600]{3,2,0,1:T(8,128)(2,1)S(1)} all-to-all(bf16[1,8,16,1600]{3,2,0,1:T(8,128)(2,1)} %bitcast.587), channel_id=1, replica_groups=mesh['pipe'=4,'dp'=16,'tensor'=8] {'tensor'}, dimensions={1} | all-to-all | bytes 819200 | tf_op jit(solution)/shard_map/all_to_all | solution.py:156
  263.2 2.2 fusion.161
  265.4 2.1 copy.231
  267.5 2.1 copy.232
  271.5 2.2 fusion.139
  273.6 7.0 collective-permute-start.16
  280.6 90.9 %collective-permute-done.16 = bf16[1,16,1600]{1,2,0:T(8,128)(2,1)} collective-permute-done((bf16[1,16,1600]{1,2,0:T(8,128)(2,1)}, bf16[1,16,1600]{1,2,0:T(8,128)(2,1)}, u32[]{:S(2)}, u32[]{:S(2)}) %collective-permute-start.16) | collective-permute-done | bytes 51232 | tf_op jit(solution)/shard_map/ppermute | solution.py:20
  373.3 15.8 %all_gather.17 = bf16[1,128,1600]{2,1,0:T(8,128)(2,1)} all-gather(bf16[1,16,1600]{2,1,0:T(8,128)(2,1)} %copy.234), channel_id=1, replica_groups=mesh['pipe'=4,'dp'=16,'tensor'=8] {'tensor'}, dimensions={1}, use_global_device_ids=true | all-gather | bytes 460800 | tf_op jit(solution)/shard_map/all_gather | solution.py:173
  391.1 2.2 bitcast_dynamic-update-slice_fusion.1
  393.2 32.0 %conditional.7 = (bf16[1,128,1600]{1,2,0:T(8,128)(2,1)}, bf16[1,1,128,768]{3,2,0,1:T(8,128)(2,1)}, bf16[1,1,128,1600]{2,3,0,1:T(8,128)(2,1)}) conditional(s32[]{:T(128)} %convert_element_type.339, () %tuple.72, (s32[]{:T(128)}, bf16[2,1,128,2,128]{4,2,3,0,1:T(8,128)(2,1)}, f32[2,1,2,128,128]{3,4,2,0,1:T(8,128)S(1)}, f32[1,1600]{1,0:T(1,128)S(1)}, ...), branch_computations={%region_11.12_spmd, %region_12.13_spmd} | conditional | flops 454803200 | bytes 11565162 | solution.py:152
  427.2 4.3 all-to-all-start.2
  440.7 4.0 all-to-all-done.2
  446.4 2.2 fusion.160
  448.6 2.1 copy.246
  450.7 2.1 copy.247
  460.1 38.8 %collective-permute-done.17 = bf16[1,16,1600]{1,2,0:T(8,128)(2,1)} collective-permute-done((bf16[1,16,1600]{1,2,0:T(8,128)(2,1)S(1)}, bf16[1,16,1600]{1,2,0:T(8,128)(2,1)}, u32[]{:S(2)}, u32[]{:S(2)}) %collective-permute-start.17) | collective-permute-done | bytes 51232 | tf_op jit(solution)/shard_map/ppermute | solution.py:20
  500.7 15.8 %all_gather.18 = bf16[1,128,1600]{2,1,0:T(8,128)(2,1)} all-gather(bf16[1,16,1600]{2,1,0:T(8,128)(2,1)} %copy.249), channel_id=1, replica_groups=mesh['pipe'=4,'dp'=16,'tensor'=8] {'tensor'}, dimensions={1}, use_global_device_ids=true | all-gather | bytes 460800 | tf_op jit(solution)/shard_map/all_gather | solution.py:173
  518.4 2.1 bitcast_dynamic-update-slice_fusion
  520.6 32.0 %conditional.8 = (bf16[1,128,1600]{1,2,0:T(8,128)(2,1)}, bf16[1,1,128,768]{3,2,0,1:T(8,128)(2,1)}, bf16[1,1,128,1600]{2,3,0,1:T(8,128)(2,1)}) conditional(s32[]{:T(128)} %convert_element_type.344, () %tuple.74, (s32[]{:T(128)}, bf16[2,1,128,2,128]{4,2,3,0,1:T(8,128)(2,1)}, f32[2,1,2,128,128]{3,4,2,0,1:T(8,128)S(1)}, f32[1,1600]{1,0:T(1,128)S(1)}, ...), branch_computations={%region_15.16_spmd, %region_16.17_spmd} | conditional | flops 454803200 | bytes 11565162 | solution.py:152
  554.6 4.1 all-to-all-start.3
  577.1 2.2 fusion.159
  579.2 2.1 copy.261
  581.3 2.1 copy.262
  585.3 2.2 fusion.129
  587.5 2.2 collective-permute-start.18
  592.9 14.5 %collective-permute-done.18 = bf16[1,16,1600]{1,2,0:T(8,128)(2,1)} collective-permute-done((bf16[1,16,1600]{1,2,0:T(8,128)(2,1)}, bf16[1,16,1600]{1,2,0:T(8,128)(2,1)}, u32[]{:S(2)}, u32[]{:S(2)}) %collective-permute-start.18) | collective-permute-done | bytes 51232 | tf_op jit(solution)/shard_map/ppermute | solution.py:20
  609.2 37.4 %all_gather.19 = bf16[1,128,1600]{2,1,0:T(8,128)(2,1)} all-gather(bf16[1,16,1600]{2,1,0:T(8,128)(2,1)} %copy.264), channel_id=1, replica_groups=mesh['pipe'=4,'dp'=16,'tensor'=8] {'tensor'}, dimensions={1}, use_global_device_ids=true | all-gather | bytes 460800 | tf_op jit(solution)/shard_map/all_gather | solution.py:173
  648.6 2.2 bitcast_dynamic-update-slice_fusion.3
  650.8 2.3 conditional.9
  653.1 2.0 copy.273
  655.1 5.3 all-to-all-start.4
  667.4 2.2 pad_maximum_fusion.5
  669.6 87.5 %fusion = bf16[112,1024]{1,0:T(8,128)(2,1)S(1)} fusion(bf16[1600,1024]{1,0:T(8,128)(2,1)} %pad_maximum_fusion.5), kind=kCustom, calls=%all-reduce-scatter | all-reduce-scatter fusion | flops 1835009 | bytes 3508224
  757.2 3.6 collective-permute-start.19
  760.7 4.1 collective-permute-start.20
  774.6 27.2 %psum.14 = f32[2,1600]{1,0:T(2,128)S(1)} all-reduce(f32[2,1600]{1,0:T(2,128)S(1)} %pad_maximum_fusion.6), channel_id=1, replica_groups=mesh['pipe'=4,'dp'=16,'tensor'=8] {'tensor'}, use_global_device_ids=true, to_apply=%region_30.31 | all-reduce | flops 3200 | bytes 25600 | tf_op jit(solution)/shard_map/psum | solution.py:192
  801.8 71.0 %psum.15 = f32[1,2,1600]{2,1,0:T(2,128)} all-reduce(f32[1,2,1600]{2,1,0:T(2,128)S(1)} %bitcast.592), channel_id=1, replica_groups=mesh['pipe'=4,'dp'=16,'tensor'=8] {'dp'}, use_global_device_ids=true, to_apply=%region_31.32 | all-reduce | flops 3200 | bytes 25600 | tf_op jit(solution)/shard_map/psum | solution.py:192
  (247 shorter events, 221.5 us)
Async XLA Ops:
  0.6 88.4 %copy-start.10 = (bf16[2,1,128,1600]{2,3,1,0:T(8,128)(2,1)S(1)}, bf16[2,1,128,1600]{2,3,1,0:T(8,128)(2,1)}, u32[]{:S(2)}) copy-start(bf16[2,1,128,1600]{2,3,1,0:T(8,128)(2,1)} %param.18) | copy-start | bytes 2457604
  1.8 12.4 %collective-permute-start = (bf16[100,1024]{1,0:T(8,128)(2,1)S(1)}, bf16[100,1024]{1,0:T(8,128)(2,1)S(1)}, u32[]{:S(2)}, u32[]{:S(2)}) collective-permute-start(bf16[100,1024]{1,0:T(8,128)(2,1)S(1)} %bitcast.589), channel_id=1, source_target_pairs={{0,8},{8,16},{16,24},{24,32},{32,40},{40,48},{48,56},{56,64},{64,7... | collective-permute-start | bytes 614408 | tf_op jit(solution)/shard_map/ppermute | solution.py:60
  5.2 10.9 %collective-permute-start.1 = (bf16[100,1024]{1,0:T(8,128)(2,1)S(1)}, bf16[100,1024]{1,0:T(8,128)(2,1)S(1)}, u32[]{:S(2)}, u32[]{:S(2)}) collective-permute-start(bf16[100,1024]{1,0:T(8,128)(2,1)S(1)} %bitcast.590), channel_id=1, source_target_pairs={{0,120},{8,0},{16,8},{24,16},{32,24},{40,32},{48,40},{56,48},{64,5... | collective-permute-start | bytes 614408 | tf_op jit(solution)/shard_map/ppermute | solution.py:65
  14.2 11.5 %collective-permute-start.2 = (bf16[100,1024]{1,0:T(8,128)(2,1)S(1)}, bf16[100,1024]{1,0:T(8,128)(2,1)S(1)}, u32[]{:S(2)}, u32[]{:S(2)}) collective-permute-start(bf16[100,1024]{1,0:T(8,128)(2,1)S(1)} %collective-permute-done), channel_id=1, source_target_pairs={{0,8},{8,16},{16,24},{24,32},{32,40},{40,48},{48,56},{56,64},{64,7... | collective-permute-start | bytes 614408 | tf_op jit(solution)/shard_map/ppermute | solution.py:60
  16.1 11.5 %collective-permute-start.3 = (bf16[100,1024]{1,0:T(8,128)(2,1)S(1)}, bf16[100,1024]{1,0:T(8,128)(2,1)S(1)}, u32[]{:S(2)}, u32[]{:S(2)}) collective-permute-start(bf16[100,1024]{1,0:T(8,128)(2,1)S(1)} %collective-permute-done.1), channel_id=1, source_target_pairs={{0,120},{8,0},{16,8},{24,16},{32,24},{40,32},{48,40},{56,48},{64,5... | collective-permute-start | bytes 614408 | tf_op jit(solution)/shard_map/ppermute | solution.py:65
  25.6 11.0 %collective-permute-start.4 = (bf16[100,1024]{1,0:T(8,128)(2,1)S(1)}, bf16[100,1024]{1,0:T(8,128)(2,1)S(1)}, u32[]{:S(2)}, u32[]{:S(2)}) collective-permute-start(bf16[100,1024]{1,0:T(8,128)(2,1)S(1)} %collective-permute-done.2), channel_id=1, source_target_pairs={{0,8},{8,16},{16,24},{24,32},{32,40},{40,48},{48,56},{56,64},{64,7... | collective-permute-start | bytes 614408 | tf_op jit(solution)/shard_map/ppermute | solution.py:60
  27.6 11.0 %collective-permute-start.5 = (bf16[100,1024]{1,0:T(8,128)(2,1)S(1)}, bf16[100,1024]{1,0:T(8,128)(2,1)S(1)}, u32[]{:S(2)}, u32[]{:S(2)}) collective-permute-start(bf16[100,1024]{1,0:T(8,128)(2,1)S(1)} %collective-permute-done.3), channel_id=1, source_target_pairs={{0,120},{8,0},{16,8},{24,16},{32,24},{40,32},{48,40},{56,48},{64,5... | collective-permute-start | bytes 614408 | tf_op jit(solution)/shard_map/ppermute | solution.py:65
  36.7 11.0 %collective-permute-start.6 = (bf16[100,1024]{1,0:T(8,128)(2,1)S(1)}, bf16[100,1024]{1,0:T(8,128)(2,1)S(1)}, u32[]{:S(2)}, u32[]{:S(2)}) collective-permute-start(bf16[100,1024]{1,0:T(8,128)(2,1)S(1)} %collective-permute-done.4), channel_id=1, source_target_pairs={{0,8},{8,16},{16,24},{24,32},{32,40},{40,48},{48,56},{56,64},{64,7... | collective-permute-start | bytes 614408 | tf_op jit(solution)/shard_map/ppermute | solution.py:60
  38.6 11.1 %collective-permute-start.7 = (bf16[100,1024]{1,0:T(8,128)(2,1)S(1)}, bf16[100,1024]{1,0:T(8,128)(2,1)}, u32[]{:S(2)}, u32[]{:S(2)}) collective-permute-start(bf16[100,1024]{1,0:T(8,128)(2,1)S(1)} %collective-permute-done.5), channel_id=1, source_target_pairs={{0,120},{8,0},{16,8},{24,16},{32,24},{40,32},{48,40},{56,48},{64,5... | collective-permute-start | bytes 614408 | tf_op jit(solution)/shard_map/ppermute | solution.py:65
  47.7 11.2 %collective-permute-start.8 = (bf16[100,1024]{1,0:T(8,128)(2,1)S(1)}, bf16[100,1024]{1,0:T(8,128)(2,1)}, u32[]{:S(2)}, u32[]{:S(2)}) collective-permute-start(bf16[100,1024]{1,0:T(8,128)(2,1)S(1)} %collective-permute-done.6), channel_id=1, source_target_pairs={{0,8},{8,16},{16,24},{24,32},{32,40},{40,48},{48,56},{56,64},{64,7... | collective-permute-start | bytes 614408 | tf_op jit(solution)/shard_map/ppermute | solution.py:60
  49.7 28.9 %collective-permute-start.9 = (bf16[100,1024]{1,0:T(8,128)(2,1)}, bf16[100,1024]{1,0:T(8,128)(2,1)}, u32[]{:S(2)}, u32[]{:S(2)}) collective-permute-start(bf16[100,1024]{1,0:T(8,128)(2,1)} %collective-permute-done.7), channel_id=1, source_target_pairs={{0,120},{8,0},{16,8},{24,16},{32,24},{40,32},{48,40},{56,48},{64,5... | collective-permute-start | bytes 614408 | tf_op jit(solution)/shard_map/ppermute | solution.py:65
  58.9 26.9 %collective-permute-start.10 = (bf16[100,1024]{1,0:T(8,128)(2,1)}, bf16[100,1024]{1,0:T(8,128)(2,1)}, u32[]{:S(2)}, u32[]{:S(2)}) collective-permute-start(bf16[100,1024]{1,0:T(8,128)(2,1)} %collective-permute-done.8), channel_id=1, source_target_pairs={{0,8},{8,16},{16,24},{24,32},{32,40},{40,48},{48,56},{56,64},{64,7... | collective-permute-start | bytes 614408 | tf_op jit(solution)/shard_map/ppermute | solution.py:60
  78.6 52.1 %copy-start = (bf16[1,2,1,128,1600]{4,3,2,1,0:T(8,128)(2,1)}, bf16[1,2,1,128,1600]{4,3,2,1,0:T(8,128)(2,1)S(1)}, u32[]{:S(2)}) copy-start(bf16[1,2,1,128,1600]{4,3,2,1,0:T(8,128)(2,1)S(1)} %all-gather) | copy-start | bytes 2457604
  78.6 11.5 %copy-start.39 = (f32[1,1600]{1,0:T(1,128)S(1)}, f32[1,1600]{1,0:T(1,128)}, u32[]{:S(2)}) copy-start(f32[1,1600]{1,0:T(1,128)} %param.20) | copy-start | bytes 19204
  78.6 15.7 %collective-permute-start.11 = (bf16[100,1024]{1,0:T(8,128)(2,1)}, bf16[100,1024]{1,0:T(8,128)(2,1)}, u32[]{:S(2)}, u32[]{:S(2)}) collective-permute-start(bf16[100,1024]{1,0:T(8,128)(2,1)} %collective-permute-done.9), channel_id=1, source_target_pairs={{0,120},{8,0},{16,8},{24,16},{32,24},{40,32},{48,40},{56,48},{64,5... | collective-permute-start | bytes 614408 | tf_op jit(solution)/shard_map/ppermute | solution.py:65
  85.8 15.7 %collective-permute-start.12 = (bf16[100,1024]{1,0:T(8,128)(2,1)}, bf16[100,1024]{1,0:T(8,128)(2,1)}, u32[]{:S(2)}, u32[]{:S(2)}) collective-permute-start(bf16[100,1024]{1,0:T(8,128)(2,1)} %collective-permute-done.10), channel_id=1, source_target_pairs={{0,8},{8,16},{16,24},{24,32},{32,40},{40,48},{48,56},{56,64},{64,7... | collective-permute-start | bytes 614408 | tf_op jit(solution)/shard_map/ppermute | solution.py:60
  94.3 32.8 %collective-permute-start.13 = (bf16[100,1024]{1,0:T(8,128)(2,1)}, bf16[100,1024]{1,0:T(8,128)(2,1)S(1)}, u32[]{:S(2)}, u32[]{:S(2)}) collective-permute-start(bf16[100,1024]{1,0:T(8,128)(2,1)} %collective-permute-done.11), channel_id=1, source_target_pairs={{0,120},{8,0},{16,8},{24,16},{32,24},{40,32},{48,40},{56,48},{64,5... | collective-permute-start | bytes 614408 | tf_op jit(solution)/shard_map/ppermute | solution.py:65
  101.5 27.4 %collective-permute-start.14 = (bf16[100,1024]{1,0:T(8,128)(2,1)}, bf16[100,1024]{1,0:T(8,128)(2,1)S(1)}, u32[]{:S(2)}, u32[]{:S(2)}) collective-permute-start(bf16[100,1024]{1,0:T(8,128)(2,1)} %collective-permute-done.12), channel_id=1, source_target_pairs={{0,8},{8,16},{16,24},{24,32},{32,40},{40,48},{48,56},{56,64},{64,7... | collective-permute-start | bytes 614408 | tf_op jit(solution)/shard_map/ppermute | solution.py:60
  103.5 27.2 %copy-start.37 = (f32[2,128]{1,0:T(2,128)}, f32[2,128]{1,0:T(2,128)S(1)}, u32[]{:S(2)}) copy-start(f32[2,128]{1,0:T(2,128)S(1)} %add_rsqrt_fusion) | copy-start | bytes 3076
  133.7 0.8 copy-start.24
  133.7 0.8 copy-start.25
  139.1 3.9 copy-start.31
  139.2 2.1 copy-start.12
  147.2 18.3 %all-to-all-start = ((bf16[1,8,16,1600]{3,2,0,1:T(8,128)(2,1)}), bf16[1,8,16,1600]{3,2,0,1:T(8,128)(2,1)}, u32[]{:S(2)}, u32[]{:S(2)}) async-start(bf16[1,8,16,1600]{3,2,0,1:T(8,128)(2,1)} %bitcast.584), calls=%async_computation | async-start | bytes 851968 | tf_op jit(solution)/shard_map/all_to_all | solution.py:156
  173.7 1.8 copy-start.2
  173.7 1.9 copy-start.6
  177.7 42.3 %collective-permute-start.15 = (bf16[1,16,1600]{1,2,0:T(8,128)(2,1)}, bf16[1,16,1600]{1,2,0:T(8,128)(2,1)}, u32[]{:S(2)}, u32[]{:S(2)}) collective-permute-start(bf16[1,16,1600]{1,2,0:T(8,128)(2,1)} %fusion.119), channel_id=1, source_target_pairs={{128,0},{256,128},{384,256},{129,1},{257,129},{385,257},{130,2},{2... | collective-permute-start | bytes 153608 | tf_op jit(solution)/shard_map/ppermute | solution.py:20
  262.6 0.6 copy-start.20
  269.6 1.8 copy-start.3
  269.6 1.9 copy-start.7
  273.6 97.9 %collective-permute-start.16 = (bf16[1,16,1600]{1,2,0:T(8,128)(2,1)}, bf16[1,16,1600]{1,2,0:T(8,128)(2,1)}, u32[]{:S(2)}, u32[]{:S(2)}) collective-permute-start(bf16[1,16,1600]{1,2,0:T(8,128)(2,1)} %fusion.139), channel_id=1, source_target_pairs={{128,0},{256,128},{384,256},{129,1},{257,129},{385,257},{130,2},{2... | collective-permute-start | bytes 153608 | tf_op jit(solution)/shard_map/ppermute | solution.py:20
  421.2 0.7 copy-start.16
  427.2 17.5 %all-to-all-start.2 = ((bf16[1,8,16,1600]{3,2,0,1:T(8,128)(2,1)}), bf16[1,8,16,1600]{3,2,0,1:T(8,128)(2,1)}, u32[]{:S(2)}, u32[]{:S(2)}) async-start(bf16[1,8,16,1600]{3,2,0,1:T(8,128)(2,1)} %bitcast.585), calls=%async_computation.2 | async-start | bytes 851968 | tf_op jit(solution)/shard_map/all_to_all | solution.py:156
  445.8 0.6 copy-start.21
  452.8 1.8 copy-start.4
  452.8 1.9 copy-start.8
  454.6 4.8 copy-start.30
  456.1 0.8 copy-start.18
  456.9 42.0 %collective-permute-start.17 = (bf16[1,16,1600]{1,2,0:T(8,128)(2,1)S(1)}, bf16[1,16,1600]{1,2,0:T(8,128)(2,1)}, u32[]{:S(2)}, u32[]{:S(2)}) collective-permute-start(bf16[1,16,1600]{1,2,0:T(8,128)(2,1)S(1)} %fusion.134), channel_id=1, source_target_pairs={{128,0},{256,128},{384,256},{129,1},{257,129},{385,257},{130,2},{2... | collective-permute-start | bytes 153608 | tf_op jit(solution)/shard_map/ppermute | solution.py:20
  548.6 0.7 copy-start.17
  554.6 20.8 %all-to-all-start.3 = ((bf16[1,8,16,1600]{3,2,0,1:T(8,128)(2,1)}), bf16[1,8,16,1600]{3,2,0,1:T(8,128)(2,1)}, u32[]{:S(2)}, u32[]{:S(2)}) async-start(bf16[1,8,16,1600]{3,2,0,1:T(8,128)(2,1)} %bitcast.586), calls=%async_computation.3 | async-start | bytes 851968 | tf_op jit(solution)/shard_map/all_to_all | solution.py:156
  576.4 0.6 copy-start.22
  583.4 1.8 copy-start.5
  583.4 1.9 copy-start.9
  587.5 19.9 %collective-permute-start.18 = (bf16[1,16,1600]{1,2,0:T(8,128)(2,1)}, bf16[1,16,1600]{1,2,0:T(8,128)(2,1)}, u32[]{:S(2)}, u32[]{:S(2)}) collective-permute-start(bf16[1,16,1600]{1,2,0:T(8,128)(2,1)} %fusion.129), channel_id=1, source_target_pairs={{128,0},{256,128},{384,256},{129,1},{257,129},{385,257},{130,2},{2... | collective-permute-start | bytes 153608 | tf_op jit(solution)/shard_map/ppermute | solution.py:20
  653.1 9.0 %copy-start.1 = (bf16[1,2,1,128,1600]{4,3,2,1,0:T(8,128)(2,1)S(1)}, bf16[1,2,1,128,1600]{4,3,2,1,0:T(8,128)(2,1)}, u32[]{:S(2)}) copy-start(bf16[1,2,1,128,1600]{4,3,2,1,0:T(8,128)(2,1)} %copy-done) | copy-start | bytes 2457604
  653.1 9.0 %copy-start.38 = (f32[2,128]{1,0:T(2,128)S(1)}, f32[2,128]{1,0:T(2,128)}, u32[]{:S(2)}) copy-start(f32[2,128]{1,0:T(2,128)} %copy-done.37) | copy-start | bytes 3076
  655.1 118.0 %all-to-all-start.4 = ((bf16[1,8,16,1600]{3,2,0,1:T(8,128)(2,1)}), bf16[1,8,16,1600]{3,2,0,1:T(8,128)(2,1)S(1)}, u32[]{:S(2)}, u32[]{:S(2)}) async-start(bf16[1,8,16,1600]{3,2,0,1:T(8,128)(2,1)} %bitcast.151), calls=%async_computation.4 | async-start | bytes 851968 | tf_op jit(solution)/shard_map/all_to_all | solution.py:156
  662.1 3.7 copy-start.11
  757.2 10.3 %collective-permute-start.19 = (bf16[112,1024]{1,0:T(8,128)(2,1)S(1)}, bf16[112,1024]{1,0:T(8,128)(2,1)S(1)}, u32[]{:S(2)}, u32[]{:S(2)}) collective-permute-start(bf16[112,1024]{1,0:T(8,128)(2,1)S(1)} %fusion), channel_id=1, source_target_pairs={{0,8},{8,16},{16,24},{24,32},{32,40},{40,48},{48,56},{56,64},{64,7... | collective-permute-start | bytes 688136
  760.7 6.8 collective-permute-start.20
  764.8 3.3 copy-start.19
  764.9 3.3 copy-start.26
  770.8 3.7 copy-start.33
  770.8 3.7 copy-start.34
  770.8 3.7 copy-start.35
  770.8 3.7 copy-start.36
  774.2 99.2 %copy-start.13 = (bf16[1,128,1600]{1,2,0:T(8,128)(2,1)S(1)}, bf16[1,128,1600]{1,2,0:T(8,128)(2,1)}, u32[]{:S(2)}) copy-start(bf16[1,128,1600]{1,2,0:T(8,128)(2,1)} %get-tuple-element.402) | copy-start | bytes 1228804
  774.2 99.2 %copy-start.40 = (f32[16]{0:T(128)S(1)}, f32[16]{0:T(128)}, u32[]{:S(2)}) copy-start(f32[16]{0:T(128)} %get-tuple-element.429) | copy-start | bytes 196
